TPU v7x, 512 devices: a whole 4x4x16 slice. The times are simulated.
512 devices in a mesh: row: 16 (over z), col: 32 (over x, y, core).
Axes of the slice: x: 4, y: 4, z: 16, core: 2. Of those that a mesh axis runs over, the one named last changes fastest.
Arguments:
- inverse_top: bfloat16 [4096, 4096], P('col', 'row'), may hold values from -0.09375 to 0.09375
- inverse_one: bfloat16 [6144, 3072], P('col', 'row'), may hold values from -0.109375 to 0.109375
- inverse_two: bfloat16 [8192, 2048], P('col', 'row'), may hold values from -0.125 to 0.125
- inverse_leaf: bfloat16 [8192, 1024], P('col', 'row'), may hold values from -0.1875 to 0.1875
- coupling_one: bfloat16 [3072, 6144], P('row', 'col'), may hold values from -0.109375 to 0.109375
- coupling_two: bfloat16 [2048, 8192], P('row', 'col'), may hold values from -0.125 to 0.125
- coupling_leaf: bfloat16 [1024, 8192], P('row', 'col'), may hold values from -0.1875 to 0.1875
- rhs_top: bfloat16 [4096, 256], P('row', 'col'), may hold values from -6 to 6
- rhs_one: bfloat16 [3072, 512], P('row', 'col'), may hold values from -6 to 6
- rhs_two: bfloat16 [2048, 1024], P('row', 'col'), may hold values from -6 to 6
- rhs_leaf: bfloat16 [1024, 2048], P('row', 'col'), may hold values from -6 to 6
- parent_map_one: int32 [2, 3072], replicated, may hold values from 0 to 4095, as said below
- parent_map_two: int32 [4, 2048], replicated, may hold values from 0 to 6143, as said below
- parent_map_leaf: int32 [8, 1024], replicated, may hold values from 0 to 4095, as said below
Outputs:
- solution_top: bfloat16 [4096, 256], P('row', 'col')
- solution_one: bfloat16 [3072, 512], P('row', 'col')
- solution_two: bfloat16 [2048, 1024], P('row', 'col')
- solution_leaf: bfloat16 [1024, 2048], P('row', 'col')
Inputs may be any that keep to these rules, and one draw needn't show every extreme that they name: `parent_map_one`: row k lists distinct rows of the top front, one for each of the 3072 update rows of front k. Cut the update rows and the top separator each into 16 equal blocks: at most 24 rows of one block land in one block of the top front, a number that is reached in every row, and every block of the top front receives exactly 192 rows from each child. `parent_map_two`: row k lists distinct rows of the front k // 2 of the second level (its 3072 separator rows first, then its 3072 update rows), one for each of the 2048 update rows of front k. Cut the update rows into 16 equal blocks, and the parent's separator rows and its update rows each into 16 equal blocks, block j of the parent being the j-th separator block with the j-th update block: at most 16 rows of one block land in one parent block, reached in every row, and every parent block receives exactly 128 rows from each child. `parent_map_leaf`: as for parent_map_two, one level lower: 1024 update rows of front k into front k // 2 of the third level, at most 8 rows of one block into one parent block, reached in every row, and exactly 64 rows from each child into every parent block.
All inputs are finite; a program needn't handle non-finite values.
Results may differ from a plain program's by a relative error of at most 0.03.
Values may be sent and summed in bfloat16 or wider, within the bound.
No kernel may reach another device: no remote copies, remote signals or barrier semaphores. Data moves between devices by JAX's collectives and lax.ppermute only.
A program may use at most 64 MiB of HBM per device.

v0:
```python
import jax
import jax.numpy as jnp
from jax import lax
from jax.sharding import PartitionSpec as P


def swapped(value, axis, stride):
    mask = 2**stride
    pairs = [(source, source ^ mask) for source in range(lax.axis_size(axis))]
    return lax.ppermute(value, axis, pairs)


def route_tables(mapping, child_index, parent_sep, parent_upd, strips, row_index):
    positions = lax.dynamic_index_in_dim(mapping, child_index, 0, keepdims=False)
    sep_rows = parent_sep // strips
    in_separator = positions < parent_sep
    if parent_upd > 0:
        upd_rows = parent_upd // strips
        target = jnp.where(
            in_separator, positions // sep_rows, (positions - parent_sep) // upd_rows
        )
        offset = jnp.where(
            in_separator, positions % sep_rows, sep_rows + (positions - parent_sep) % upd_rows
        )
    else:
        target = positions // sep_rows
        offset = positions % sep_rows
    block_rows = positions.shape[0] // strips
    blocks = target.reshape(strips, block_rows)
    matches = (blocks[:, :, None] == jnp.arange(strips, dtype=jnp.int32)[None, None, :]).astype(
        jnp.int32
    )
    slot_of = jnp.sum((jnp.cumsum(matches, axis=1) - 1) * matches, axis=2).reshape(-1)
    block_len = sep_rows + parent_upd // strips
    capacity = 2 * positions.shape[0] // (strips * strips)
    source = jnp.arange(positions.shape[0], dtype=jnp.int32) // block_rows
    mine_here = target == row_index
    column_at = jnp.where(mine_here, slot_of, capacity)
    lookup = jnp.full((strips, capacity + 1), block_len, jnp.int32)
    lookup = lookup.at[source, column_at].set(jnp.where(mine_here, offset, block_len))[:, :capacity]
    local_target = lax.dynamic_slice_in_dim(target, row_index * block_rows, block_rows)
    local_slots = lax.dynamic_slice_in_dim(slot_of, row_index * block_rows, block_rows)
    return (local_target, local_slots, lookup, capacity, block_len)


def pack_rows(values, local_target, local_slots, strips, capacity):
    buffer = jnp.zeros((strips, capacity, values.shape[1]), values.dtype)
    return buffer.at[local_target, local_slots].set(values)


def unpack_rows(received, lookup, block_len):
    summed = jnp.zeros((block_len + 1, received.shape[2]), jnp.float32)
    return summed.at[lookup].add(received.astype(jnp.float32))[:block_len]


def spread(portion, depth_bits, pass_on, column):
    for bit_index in range(depth_bits):
        partner = pass_on(portion, bit_index)
        is_upper = column >> bit_index & 1 == 1
        portion = jnp.where(
            is_upper,
            jnp.concatenate([partner, portion], axis=-1),
            jnp.concatenate([portion, partner], axis=-1),
        )
    return portion


def shrink(entire, depth_bits, pass_on, column):
    for bit_index in reversed(range(depth_bits)):
        half_width = entire.shape[-1] // 2
        low_part = entire[..., :half_width]
        high_part = entire[..., half_width:]
        is_upper = column >> bit_index & 1 == 1
        kept_part = jnp.where(is_upper, high_part, low_part)
        sent_part = jnp.where(is_upper, low_part, high_part)
        entire = kept_part + pass_on(sent_part, bit_index)
    return entire


def per_device(
    inverse_top,
    inverse_one,
    inverse_two,
    inverse_leaf,
    coupling_one,
    coupling_two,
    coupling_leaf,
    rhs_top,
    rhs_one,
    rhs_two,
    rhs_leaf,
    parent_map_one,
    parent_map_two,
    parent_map_leaf,
):
    strips = lax.axis_size("row")
    col_count = lax.axis_size("col")
    row_here = lax.axis_index("row")
    column = lax.axis_index("col")
    inverses = [inverse_top, inverse_one, inverse_two, inverse_leaf]
    couplings = [None, coupling_one, coupling_two, coupling_leaf]
    right_sides = [rhs_top, rhs_one, rhs_two, rhs_leaf]
    parent_maps = [None, parent_map_one, parent_map_two, parent_map_leaf]
    orders = [inverse.shape[1] * strips for inverse in inverses]
    groups = [col_count >> tree_level for tree_level in range(4)]
    group_bits = [group_size.bit_length() - 1 for group_size in groups]
    pass_rhs = lambda values, bit_index: swapped(values, "col", bit_index)
    pass_update_sum = lambda values, bit_index: swapped(
        values.astype(jnp.bfloat16), "col", bit_index
    ).astype(values.dtype)
    pass_update_spread = lambda values, bit_index: swapped(values, "col", bit_index)
    pass_solution_sum = lambda values, bit_index: swapped(
        values.astype(jnp.bfloat16), "col", bit_index
    ).astype(values.dtype)
    pass_solution_spread = lambda values, bit_index: swapped(values, "col", bit_index)
    full_rhs = [
        spread(right_sides[tree_level], group_bits[tree_level], pass_rhs, column)
        for tree_level in range(4)
    ]
    own_routes = [None]
    sibling_routes = [None]
    for tree_level in range(1, 4):
        parent_order = orders[tree_level - 1]
        parent_update = parent_order if tree_level > 1 else 0
        front_here = column // groups[tree_level]
        own_routes.append(
            route_tables(
                parent_maps[tree_level], front_here, parent_order, parent_update, strips, row_here
            )
        )
        sibling_routes.append(
            route_tables(
                parent_maps[tree_level],
                front_here ^ 1,
                parent_order,
                parent_update,
                strips,
                row_here,
            )
        )
    pivots = [None] * 4
    incoming = None
    for tree_level in (3, 2, 1, 0):
        sep_rows = inverses[tree_level].shape[1]
        if incoming is None:
            separator = full_rhs[tree_level]
            own_update = None
        else:
            separator = (full_rhs[tree_level].astype(jnp.float32) + incoming[:sep_rows]).astype(
                jnp.bfloat16
            )
            own_update = lax.optimization_barrier(incoming[sep_rows:].astype(jnp.bfloat16))
        partial_value = jnp.dot(inverses[tree_level], separator, preferred_element_type=jnp.float32)
        solved = lax.psum(partial_value.astype(jnp.bfloat16), "row")
        pivots[tree_level] = solved
        if tree_level > 0:
            coupled = jnp.dot(couplings[tree_level], solved, preferred_element_type=jnp.float32)
            reduced = shrink(coupled, group_bits[tree_level], pass_update_sum, column)
            if own_update is None:
                portion = (-reduced).astype(jnp.bfloat16)
            else:
                start_at = column % groups[tree_level] * reduced.shape[1]
                kept_rows = lax.dynamic_slice_in_dim(own_update, start_at, reduced.shape[1], 1)
                portion = (kept_rows.astype(jnp.float32) - reduced).astype(jnp.bfloat16)
            updated = spread(portion, group_bits[tree_level], pass_update_spread, column)
            own_target, own_slots, own_lookup, capacity, block_len = own_routes[tree_level]
            partner = swapped(updated, "col", group_bits[tree_level])
            sib_target, sib_slots, sib_lookup = sibling_routes[tree_level][:3]
            got_own, got_sibling = (
                lax.all_to_all(
                    pack_rows(updated, own_target, own_slots, strips, capacity),
                    "row",
                    split_axis=0,
                    concat_axis=0,
                    tiled=True,
                ),
                lax.all_to_all(
                    pack_rows(partner, sib_target, sib_slots, strips, capacity),
                    "row",
                    split_axis=0,
                    concat_axis=0,
                    tiled=True,
                ),
            )
            incoming = unpack_rows(got_own, own_lookup, block_len) + unpack_rows(
                got_sibling, sib_lookup, block_len
            )
    solutions = [None] * 4
    parent_solution = None
    parent_gathered = None
    for tree_level in range(4):
        solved = pivots[tree_level]
        gathered = None
        if tree_level == 0:
            residual = solved
        else:
            own_target, own_slots, own_lookup, capacity, block_len = own_routes[tree_level]
            pieces = [parent_solution]
            if parent_gathered is not None:
                pieces.append(parent_gathered)
            pieces.append(jnp.zeros((1, parent_solution.shape[1]), jnp.bfloat16))
            parent_rows = jnp.concatenate(pieces, axis=0)
            returned = lax.all_to_all(
                parent_rows[own_lookup], "row", split_axis=0, concat_axis=0, tiled=True
            )
            gathered = returned[own_target, own_slots]
            coupling_term = jnp.dot(
                couplings[tree_level].T, gathered, preferred_element_type=jnp.float32
            )
            residual = (
                solved.astype(jnp.float32)
                - lax.psum(coupling_term.astype(jnp.bfloat16), "row").astype(jnp.float32)
            ).astype(jnp.bfloat16)
        contribution = jnp.dot(inverses[tree_level].T, residual, preferred_element_type=jnp.float32)
        if tree_level == 0:
            summed = lax.psum(contribution.astype(jnp.bfloat16), "col")
            solution = summed
            rhs_width = solution.shape[1] // groups[0]
            solutions[0] = lax.dynamic_slice_in_dim(
                solution, column % groups[0] * rhs_width, rhs_width, 1
            )
        else:
            portion = shrink(
                contribution, group_bits[tree_level], pass_solution_sum, column
            ).astype(jnp.bfloat16)
            solutions[tree_level] = portion
            if tree_level < 3:
                solution = spread(portion, group_bits[tree_level], pass_solution_spread, column)
        parent_solution = solution
        parent_gathered = gathered
    return (solutions[0], solutions[1], solutions[2], solutions[3])


def solution(mesh):
    in_specs = (
        P("col", "row"),
        P("col", "row"),
        P("col", "row"),
        P("col", "row"),
        P("row", "col"),
        P("row", "col"),
        P("row", "col"),
        P("row", "col"),
        P("row", "col"),
        P("row", "col"),
        P("row", "col"),
        P(),
        P(),
        P(),
    )
    out_specs = (P("row", "col"), P("row", "col"), P("row", "col"), P("row", "col"))
    return jax.shard_map(
        per_device, mesh=mesh, in_specs=in_specs, out_specs=out_specs, check_vma=False
    )
```

profile of v0, /device:TPU:1, one launch (start us, length us, event | category | flops | bytes accessed | tf_op | source)
XLA Modules:
  0.0 1660.7 jit_solution(15482872862704650823)
XLA Ops:
  7.2 8.8 collective-permute-start.5
  37.4 9.1 reduce-window.14
  54.5 124.7 %all-reduce.12.cloned.1.call-done = bf16[256,256]{0,1:T(8,128)(2,1)} async-done(((bf16[256,256]{0,1:T(8,128)(2,1)}), bf16[256,256]{0,1:T(8,128)(2,1)}) %all-reduce.12.cloned.1.call-update) | async-done | bytes 131088 | tf_op jit(solution)/shard_map/psum | solution.py:154
  185.4 12.4 collective-permute-start.8
  197.7 4.3 scatter_custom_fusion.15
  210.5 7.7 scatter_fusion
  218.2 7.7 all-to-all-start
  230.5 4.7 collective-permute-start.11
  238.1 7.7 scatter_fusion.1
  245.8 11.6 all-to-all-start.1
  261.5 9.1 reduce-window.16
  275.7 127.6 %all-reduce.14.cloned.1.call-done = bf16[256,256]{0,1:T(8,128)(2,1)} async-done(((bf16[256,256]{0,1:T(8,128)(2,1)}), bf16[256,256]{0,1:T(8,128)(2,1)}) %all-reduce.14.cloned.1.call-update) | async-done | bytes 131088 | tf_op jit(solution)/shard_map/psum | solution.py:154
  404.4 4.6 collective-permute-start.15
  415.2 13.9 collective-permute-start.17
  432.2 8.0 scatter_custom_fusion.13
  444.8 4.6 collective-permute-start.20
  449.5 8.0 scatter_custom_fusion.16
  458.5 15.0 scatter_fusion.2
  473.5 7.6 all-to-all-start.2
  487.2 15.0 scatter_fusion.3
  502.2 11.7 all-to-all-start.3
  535.0 128.0 %all-reduce.16.cloned.1.call-done = bf16[192,256]{1,0:T(8,128)(2,1)} async-done(((bf16[192,256]{1,0:T(8,128)(2,1)}), bf16[192,256]{1,0:T(8,128)(2,1)}) %all-reduce.16.cloned.1.call-update) | async-done | bytes 98320 | tf_op jit(solution)/shard_map/psum | solution.py:154
  669.5 4.6 collective-permute-start.27
  681.0 15.2 collective-permute-start.29
  705.4 4.6 collective-permute-start.32
  717.4 22.2 %scatter_fusion.4 = bf16[16,24,256]{2,1,0:T(8,128)(2,1)} fusion(bf16[16,24,256]{2,1,0:T(8,128)(2,1)} %broadcast.1392.clone.1, s32[192]{0:T(256)S(1)} %bitcast.300, bf16[192,256]{1,0:T(8,128)(2,1)S(1)} %maximum_select_fusion.4), kind=kCustom, calls=%fused_computation.14 | custom fusion | bytes 296448 | tf_op jit(solution)/shard_map/scatter | solution.py:48
  739.6 6.4 all-to-all-start.4
  751.4 4.8 collective-permute-start.34
  756.1 4.6 collective-permute-start.2
  761.5 22.1 %scatter_fusion.5 = bf16[16,24,256]{2,1,0:T(8,128)(2,1)} fusion(bf16[16,24,256]{2,1,0:T(8,128)(2,1)} %broadcast.1392.clone, s32[192]{0:T(256)S(1)} %bitcast.299, bf16[192,256]{1,0:T(8,128)(2,1)S(1)} %collective-permute-done.34), kind=kCustom, calls=%fused_computation.16 | custom fusion | bytes 296448 | tf_op jit(solution)/shard_map/scatter | solution.py:48
  783.6 11.7 all-to-all-start.5
  795.3 11.8 scatter_custom_fusion.12
  809.6 11.8 scatter_custom_fusion.17
  832.0 127.1 %all-reduce.18.cloned.1.call-done = bf16[128,256]{0,1:T(8,128)(2,1)} async-done(((bf16[128,256]{0,1:T(8,128)(2,1)}), bf16[128,256]{0,1:T(8,128)(2,1)}) %all-reduce.18.cloned.1.call-update) | async-done | bytes 65552 | tf_op jit(solution)/shard_map/psum | solution.py:154
  960.8 138.6 %all-reduce.20.cloned.1.call-done = bf16[256,256]{0,1:T(8,128)(2,1)} async-done(((bf16[256,256]{0,1:T(8,128)(2,1)}), bf16[256,256]{0,1:T(8,128)(2,1)}) %all-reduce.20.cloned.1.call-update) | async-done | bytes 131088 | tf_op jit(solution)/shard_map/psum | solution.py:216
  1102.5 24.2 %all_to_all.45 = bf16[16,24,256]{2,1,0:T(8,128)(2,1)S(1)} all-to-all(bf16[16,24,256]{2,1,0:T(8,128)(2,1)S(1)} %bitcast.302), channel_id=1, replica_groups=mesh['row'=16,'col'=32] {'row'}, dimensions={0} | all-to-all | bytes 393216 | tf_op jit(solution)/shard_map/all_to_all | solution.py:203
  1130.0 121.3 %all-reduce.22.cloned.1.call-done = bf16[192,256]{1,0:T(8,128)(2,1)} async-done(((bf16[192,256]{1,0:T(8,128)(2,1)}), bf16[192,256]{1,0:T(8,128)(2,1)}) %all-reduce.22.cloned.1.call-update) | async-done | bytes 98320 | tf_op jit(solution)/shard_map/psum | solution.py:212
  1257.8 4.6 collective-permute-start.36
  1269.4 15.2 collective-permute-start.38
  1293.8 4.6 collective-permute-start.41
  1306.3 18.2 %all_to_all.46 = bf16[16,16,256]{2,1,0:T(8,128)(2,1)S(1)} all-to-all(bf16[16,16,256]{2,1,0:T(8,128)(2,1)S(1)} %bitcast.307), channel_id=1, replica_groups=mesh['row'=16,'col'=32] {'row'}, dimensions={0} | all-to-all | bytes 262144 | tf_op jit(solution)/shard_map/all_to_all | solution.py:203
  1326.6 123.0 %all-reduce.24.cloned.1.call-done = bf16[256,256]{0,1:T(8,128)(2,1)} async-done(((bf16[256,256]{0,1:T(8,128)(2,1)}), bf16[256,256]{0,1:T(8,128)(2,1)}) %all-reduce.24.cloned.1.call-update) | async-done | bytes 131088 | tf_op jit(solution)/shard_map/psum | solution.py:212
  1450.7 4.6 collective-permute-start.43
  1461.4 13.9 collective-permute-start.45
  1483.7 4.6 collective-permute-start.48
  1490.9 19.0 %all_to_all.47 = bf16[16,8,256]{2,1,0:T(8,128)(2,1)S(1)} all-to-all(bf16[16,8,256]{2,1,0:T(8,128)(2,1)S(1)} %bitcast.308), channel_id=1, replica_groups=mesh['row'=16,'col'=32] {'row'}, dimensions={0} | all-to-all | bytes 131072 | tf_op jit(solution)/shard_map/all_to_all | solution.py:203
  1511.7 120.9 %all-reduce.26.cloned.1.call-done = bf16[256,256]{0,1:T(8,128)(2,1)} async-done(((bf16[256,256]{0,1:T(8,128)(2,1)}), bf16[256,256]{0,1:T(8,128)(2,1)}) %all-reduce.26.cloned.1.call-update) | async-done | bytes 131088 | tf_op jit(solution)/shard_map/psum | solution.py:212
  1638.6 12.4 collective-permute-start.50
  (384 shorter events, 220.3 us)
Async XLA Ops:
  7.2 172.1 %all-reduce.12.cloned.1.call-start = ((), (), s32[]{:S(2)}) async-start(), calls=%async_computation.9 | async-start | bytes 262144 | tf_op jit(solution)/shard_map/psum | solution.py:154
  7.2 40.5 %collective-permute-start.5 = (bf16[64,64]{1,0:T(8,128)(2,1)}, bf16[64,64]{1,0:T(8,128)(2,1)S(1)}, u32[]{:S(2)}, u32[]{:S(2)}) collective-permute-start(bf16[64,64]{1,0:T(8,128)(2,1)} %param.24), channel_id=1, source_target_pairs={{0,1},{1,0},{2,3},{3,2},{4,5},{5,4},{6,7},{7,6},{8,9},{9,8},{10,11... | collective-permute-start | bytes 24584 | tf_op jit(solution)/shard_map/ppermute | solution.py:10
  16.0 219.2 %collective-permute-start.12 = (bf16[128,32]{0,1:T(8,128)(2,1)}, bf16[128,32]{0,1:T(8,128)(2,1)S(1)}, u32[]{:S(2)}, u32[]{:S(2)}) collective-permute-start(bf16[128,32]{0,1:T(8,128)(2,1)} %param.23), channel_id=1, source_target_pairs={{0,1},{1,0},{2,3},{3,2},{4,5},{5,4},{6,7},{7,6},{8,9},{9,8},{10,11... | collective-permute-start | bytes 24584 | tf_op jit(solution)/shard_map/ppermute | solution.py:10
  18.0 466.7 %collective-permute-start.22 = (bf16[192,16]{0,1:T(8,128)(2,1)}, bf16[192,16]{0,1:T(8,128)(2,1)S(1)}, u32[]{:S(2)}, u32[]{:S(2)}) collective-permute-start(bf16[192,16]{0,1:T(8,128)(2,1)} %param.22), channel_id=1, source_target_pairs={{0,1},{1,0},{2,3},{3,2},{4,5},{5,4},{6,7},{7,6},{8,9},{9,8},{10,11... | collective-permute-start | bytes 18440 | tf_op jit(solution)/shard_map/ppermute | solution.py:10
  20.4 725.8 %collective-permute-start = (bf16[256,8]{0,1:T(8,128)(2,1)}, bf16[256,8]{0,1:T(8,128)(2,1)S(1)}, u32[]{:S(2)}, u32[]{:S(2)}) collective-permute-start(bf16[256,8]{0,1:T(8,128)(2,1)} %param.21), channel_id=1, source_target_pairs={{0,1},{1,0},{2,3},{3,2},{4,5},{5,4},{6,7},{7,6},{8,9},{9,8},{10,11... | collective-permute-start | bytes 12296 | tf_op jit(solution)/shard_map/ppermute | solution.py:10
  180.4 4.9 collective-permute-start.7
  185.4 16.8 %collective-permute-start.8 = (bf16[64,64]{1,0:T(8,128)(2,1)S(1)}, bf16[64,64]{1,0:T(8,128)(2,1)S(1)}, u32[]{:S(2)}, u32[]{:S(2)}) collective-permute-start(bf16[64,64]{1,0:T(8,128)(2,1)S(1)} %select_convert_fusion.14), channel_id=1, source_target_pairs={{0,1},{1,0},{2,3},{3,2},{4,5},{5,4},{6,7},{7,6},{8,9},{9,8},{10,11... | collective-permute-start | bytes 24584 | tf_op jit(solution)/shard_map/ppermute | solution.py:10
  218.2 27.6 %all-to-all-start = ((bf16[16,8,256]{2,1,0:T(8,128)(2,1)}), bf16[16,8,256]{2,1,0:T(8,128)(2,1)S(1)}, u32[]{:S(2)}, u32[]{:S(2)}) async-start(bf16[16,8,256]{2,1,0:T(8,128)(2,1)} %scatter_fusion), calls=%async_computation | async-start | bytes 131072 | tf_op jit(solution)/shard_map/all_to_all | solution.py:170
  230.5 6.9 collective-permute-start.11
  235.2 22.2 %collective-permute-start.13 = (bf16[128,64]{0,1:T(8,128)(2,1)S(1)}, bf16[128,64]{0,1:T(8,128)(2,1)S(1)}, u32[]{:S(2)}, u32[]{:S(2)}) collective-permute-start(bf16[128,64]{0,1:T(8,128)(2,1)S(1)} %maximum_select_fusion.28), channel_id=1, source_target_pairs={{0,2},{1,3},{2,0},{3,1},{4,6},{5,7},{6,4},{7,5},{8,10},{9,11},{10,... | collective-permute-start | bytes 49160 | tf_op jit(solution)/shard_map/ppermute | solution.py:10
  245.8 26.7 %all-to-all-start.1 = ((bf16[16,8,256]{2,1,0:T(8,128)(2,1)}), bf16[16,8,256]{2,1,0:T(8,128)(2,1)S(1)}, u32[]{:S(2)}, u32[]{:S(2)}) async-start(bf16[16,8,256]{2,1,0:T(8,128)(2,1)} %scatter_fusion.1), calls=%async_computation.1 | async-start | bytes 131072 | tf_op jit(solution)/shard_map/all_to_all | solution.py:177
  257.4 145.9 %all-reduce.14.cloned.1.call-start = ((), (), s32[]{:S(2)}) async-start(), calls=%async_computation.10 | async-start | bytes 262144 | tf_op jit(solution)/shard_map/psum | solution.py:154
  257.5 16.6 collective-permute-start.14
  404.4 6.2 collective-permute-start.15
  415.2 14.7 collective-permute-start.17
  429.9 10.4 collective-permute-start.18
  444.8 12.9 collective-permute-start.20
  473.5 28.7 %all-to-all-start.2 = ((bf16[16,16,256]{2,1,0:T(8,128)(2,1)}), bf16[16,16,256]{2,1,0:T(8,128)(2,1)S(1)}, u32[]{:S(2)}, u32[]{:S(2)}) async-start(bf16[16,16,256]{2,1,0:T(8,128)(2,1)} %scatter_fusion.2), calls=%async_computation.2 | async-start | bytes 262144 | tf_op jit(solution)/shard_map/all_to_all | solution.py:170
  481.4 5.0 collective-permute-start.21
  502.2 28.9 %all-to-all-start.3 = ((bf16[16,16,256]{2,1,0:T(8,128)(2,1)}), bf16[16,16,256]{2,1,0:T(8,128)(2,1)S(1)}, u32[]{:S(2)}, u32[]{:S(2)}) async-start(bf16[16,16,256]{2,1,0:T(8,128)(2,1)} %scatter_fusion.3), calls=%async_computation.3 | async-start | bytes 262144 | tf_op jit(solution)/shard_map/all_to_all | solution.py:177
  513.9 149.2 %all-reduce.16.cloned.1.call-start = ((), (), s32[]{:S(2)}) async-start(), calls=%async_computation.11 | async-start | bytes 196608 | tf_op jit(solution)/shard_map/psum | solution.py:154
  514.0 4.8 collective-permute-start.23
  518.9 6.6 collective-permute-start.24
  525.6 7.6 collective-permute-start.25
  664.1 5.2 collective-permute-start.26
  669.5 6.3 collective-permute-start.27
  681.0 16.1 collective-permute-start.29
  705.4 6.3 collective-permute-start.32
  739.6 44.0 %all-to-all-start.4 = ((bf16[16,24,256]{2,1,0:T(8,128)(2,1)}), bf16[16,24,256]{2,1,0:T(8,128)(2,1)S(1)}, u32[]{:S(2)}, u32[]{:S(2)}) async-start(bf16[16,24,256]{2,1,0:T(8,128)(2,1)} %scatter_fusion.4), calls=%async_computation.4 | async-start | bytes 393216 | tf_op jit(solution)/shard_map/all_to_all | solution.py:170
  751.4 9.4 collective-permute-start.34
  756.1 51.1 %collective-permute-start.2 = (bf16[256,32]{1,0:T(8,128)(2,1)S(1)}, bf16[256,32]{1,0:T(8,128)(2,1)S(1)}, u32[]{:S(2)}, u32[]{:S(2)}) collective-permute-start(bf16[256,32]{1,0:T(8,128)(2,1)S(1)} %broadcast_select_fusion), channel_id=1, source_target_pairs={{0,4},{1,5},{2,6},{3,7},{4,0},{5,1},{6,2},{7,3},{8,12},{9,13},{10,... | collective-permute-start | bytes 49160 | tf_op jit(solution)/shard_map/ppermute | solution.py:10
  783.6 44.6 %all-to-all-start.5 = ((bf16[16,24,256]{2,1,0:T(8,128)(2,1)}), bf16[16,24,256]{2,1,0:T(8,128)(2,1)S(1)}, u32[]{:S(2)}, u32[]{:S(2)}) async-start(bf16[16,24,256]{2,1,0:T(8,128)(2,1)} %scatter_fusion.5), calls=%async_computation.5 | async-start | bytes 393216 | tf_op jit(solution)/shard_map/all_to_all | solution.py:177
  795.3 163.8 %all-reduce.18.cloned.1.call-start = ((), (), s32[]{:S(2)}) async-start(), calls=%async_computation.12 | async-start | bytes 131072 | tf_op jit(solution)/shard_map/psum | solution.py:154
  807.3 14.1 collective-permute-start.3
  821.6 9.5 collective-permute-start.4
  831.9 267.5 %all-reduce.20.cloned.1.call-start = ((), (), s32[]{:S(2)}) async-start(), calls=%async_computation.13 | async-start | bytes 262144 | tf_op jit(solution)/shard_map/psum | solution.py:216
  960.8 290.6 %all-reduce.22.cloned.1.call-start = ((), (), s32[]{:S(2)}) async-start(), calls=%async_computation.14 | async-start | bytes 196608 | tf_op jit(solution)/shard_map/psum | solution.py:212
  1130.0 319.6 %all-reduce.24.cloned.1.call-start = ((), (), s32[]{:S(2)}) async-start(), calls=%async_computation.15 | async-start | bytes 262144 | tf_op jit(solution)/shard_map/psum | solution.py:212
  1252.5 5.2 collective-permute-start.35
  1257.8 6.3 collective-permute-start.36
  1269.4 16.1 collective-permute-start.38
  1293.8 6.3 collective-permute-start.41
  1326.6 306.0 %all-reduce.26.cloned.1.call-start = ((), (), s32[]{:S(2)}) async-start(), calls=%async_computation.16 | async-start | bytes 262144 | tf_op jit(solution)/shard_map/psum | solution.py:212
  1450.7 6.2 collective-permute-start.43
  1461.4 14.7 collective-permute-start.45
  1483.7 6.2 collective-permute-start.48
  1633.6 4.9 collective-permute-start.49
  1638.6 14.3 collective-permute-start.50
  (40 other events, 1395.3 us)
Sparse Core Ops, SparseCore 0:
  53.8 125.3 all-reduce.11
  275.8 127.4 all-reduce.13
  535.0 128.0 all-reduce.15
  832.1 126.9 all-reduce.17
  962.1 137.2 all-reduce.19
  1130.1 121.2 all-reduce.21
  1326.7 122.8 all-reduce.23
  1511.8 120.6 all-reduce.25
where the time goes:
time: 1670 us; the launch traced here: 1660 us
  waiting for transfers between devices  1060 us (63%)
  starting transfers between devices  293 us (18%)
  local copies, waits for them, and re-layouts  168 us (10%)
  blocking collectives  61.5 us (4%)
  other arithmetic  46.3 us (3%)
    psum x4, waiting for transfers between devices, per_device(): solved = lax.psum(partial_value.astype(jnp.bfloat16), 'row')  507 us
    psum x3, waiting for transfers between devices, per_device(): lax.psum(coupling_term.astype(jnp.bfloat16), 'row').astype(jnp.float32)  365 us
    ppermute x51, starting transfers between devices, swapped(): return lax.ppermute(value, axis, pairs)  236 us
    psum x1, waiting for transfers between devices, per_device(): summed = lax.psum(contribution.astype(jnp.bfloat16), 'col')  139 us
    scatter x6, local copies, waits for them, and re-layouts, pack_rows(): return buffer.at[local_target, local_slots].set(values)  89.7 us
    all_to_all x3, blocking collectives, per_device(): lax.all_to_all(parent_rows[own_lookup], 'row', split_axis=0, concat_axis=...  61.5 us
    unnamed x56, local copies, waits for them, and re-layouts  56.3 us
    ppermute x51, waiting for transfers between devices, swapped(): return lax.ppermute(value, axis, pairs)  50.9 us
  transfers between devices with their start and end apart: 65, of which 42 were waited for; matrix products, arithmetic and copies ran while one was open for 12% of the time, Pallas kernels for 0%

commit v1 on v0

--- a/solution.py
+++ b/solution.py
@@ -151,7 +151,7 @@
             )
             own_update = lax.optimization_barrier(incoming[sep_rows:].astype(jnp.bfloat16))
         partial_value = jnp.dot(inverses[tree_level], separator, preferred_element_type=jnp.float32)
-        solved = lax.psum(partial_value.astype(jnp.bfloat16), "row")
+        solved = jnp.sum(lax.all_gather(partial_value.astype(jnp.bfloat16), "row"), axis=0)
         pivots[tree_level] = solved
         if tree_level > 0:
             coupled = jnp.dot(couplings[tree_level], solved, preferred_element_type=jnp.float32)

time: 1670 us -> 1400 us (0.84)
  waiting for transfers between devices: 1060 us -> 778 us
    psum x4 -> x0, waiting for transfers between devices: 507 us -> none  [per_device(): solved = lax.psum(partial_value.astype(jnp.bfloat16), 'row')]
    all_gather x0 -> x4, waiting for transfers between devices: none -> 219 us  [per_device(): lax.all_gather(partial_value.astype(jnp.bfloat16), 'row')]
    unnamed x56 -> x49, local copies, waits for them, and re-layouts: 56.3 us -> 56.1 us
  transfers between devices with their start and end apart: 65 -> 65, of which waited for: 42 -> 45; matrix products, arithmetic and copies ran while one was open for 12% -> 15% of each run, Pallas kernels for 0% -> 0%
where the time goes in v1:
time: 1400 us; the launch traced here: 1390 us
  waiting for transfers between devices  778 us (56%)
  starting transfers between devices  300 us (21%)
  local copies, waits for them, and re-layouts  167 us (12%)
  blocking collectives  61.5 us (4%)
  other arithmetic  52.2 us (4%)
  between operations  16.3 us (1%)
    psum x3, waiting for transfers between devices, per_device(): lax.psum(coupling_term.astype(jnp.bfloat16), 'row').astype(jnp.float32)  365 us
    ppermute x51, starting transfers between devices, swapped(): return lax.ppermute(value, axis, pairs)  243 us
    all_gather x4, waiting for transfers between devices, per_device(): lax.all_gather(partial_value.astype(jnp.bfloat16), 'row')  219 us
    psum x1, waiting for transfers between devices, per_device(): summed = lax.psum(contribution.astype(jnp.bfloat16), 'col')  138 us
    scatter x6, local copies, waits for them, and re-layouts, pack_rows(): return buffer.at[local_target, local_slots].set(values)  89.7 us
    all_to_all x3, blocking collectives, per_device(): lax.all_to_all(parent_rows[own_lookup], 'row', split_axis=0, concat_axis=...  61.5 us
    unnamed x49, local copies, waits for them, and re-layouts  56.1 us
    ppermute x51, waiting for transfers between devices, swapped(): return lax.ppermute(value, axis, pairs)  47.9 us
  transfers between devices with their start and end apart: 65, of which 45 were waited for; matrix products, arithmetic and copies ran while one was open for 15% of the time, Pallas kernels for 0%

profile of v1, /device:TPU:1, one launch (start us, length us, event | category | flops | bytes accessed | tf_op | source)
XLA Modules:
  0.0 1386.6 jit_solution(16436757630806562708)
XLA Ops:
  7.2 8.8 collective-permute-start.5
  34.0 58.9 %all-gather.9.cloned.1.call-done = bf16[4096,256]{0,1:T(8,128)(2,1)} async-done(((bf16[256,256]{0,1:T(8,128)(2,1)}), bf16[4096,256]{0,1:T(8,128)(2,1)}) %all-gather.9.cloned.1.call-update) | async-done | bytes 2097168 | tf_op jit(solution)/shard_map/all_gather | solution.py:154
  101.1 13.7 collective-permute-start.8
  127.6 7.7 scatter_fusion
  135.3 7.1 all-to-all-start
  155.2 7.7 scatter_fusion.1
  162.8 11.6 all-to-all-start.1
  178.5 7.5 all-to-all-done.1
  188.6 5.9 collective-permute-start.22
  204.2 48.8 %all-gather.11.cloned.1.call-done = bf16[4096,256]{0,1:T(8,128)(2,1)} async-done(((bf16[256,256]{0,1:T(8,128)(2,1)}), bf16[4096,256]{0,1:T(8,128)(2,1)}) %all-gather.11.cloned.1.call-update) | async-done | bytes 2097168 | tf_op jit(solution)/shard_map/all_gather | solution.py:154
  256.7 4.6 collective-permute-start.15
  267.4 14.8 %collective-permute-start.17 = (bf16[128,32]{0,1:T(8,128)(2,1)S(1)}, bf16[128,32]{0,1:T(8,128)(2,1)S(1)}, u32[]{:S(2)}, u32[]{:S(2)}) collective-permute-start(bf16[128,32]{0,1:T(8,128)(2,1)S(1)} %select_convert_fusion.17), channel_id=1, source_target_pairs={{0,1},{1,0},{2,3},{3,2},{4,5},{5,4},{6,7},{7,6},{8,9},{9,8},{10,11... | collective-permute-start | bytes 24584 | tf_op jit(solution)/shard_map/ppermute | solution.py:10
  290.6 4.6 collective-permute-start.20
  295.3 8.0 scatter_custom_fusion.13
  304.3 15.0 %scatter_fusion.2 = bf16[16,16,256]{2,1,0:T(8,128)(2,1)} fusion(bf16[16,16,256]{2,1,0:T(8,128)(2,1)} %broadcast.1409.clone.1, s32[128]{0:T(128)S(1)} %get-tuple-element.77, bf16[128,256]{1,0:T(8,128)(2,1)S(1)} %copy.212), kind=kCustom, calls=%fused_computation.10 | custom fusion | bytes 197632 | tf_op jit(solution)/shard_map/scatter | solution.py:48
  319.3 7.2 all-to-all-start.2
  326.6 8.0 scatter_custom_fusion.16
  341.2 15.0 %scatter_fusion.3 = bf16[16,16,256]{2,1,0:T(8,128)(2,1)} fusion(bf16[16,16,256]{2,1,0:T(8,128)(2,1)} %broadcast.1409.clone, s32[128]{0:T(128)S(1)} %fusion.156, bf16[128,256]{1,0:T(8,128)(2,1)S(1)} %copy.222), kind=kCustom, calls=%fused_computation.12 | custom fusion | bytes 197632 | tf_op jit(solution)/shard_map/scatter | solution.py:48
  356.2 11.5 all-to-all-start.3
  382.8 9.1 reduce-window.14
  392.9 9.1 reduce-window.16
  402.9 45.3 %all-gather.13.cloned.1.call-done = bf16[3072,256]{1,0:T(8,128)(2,1)} async-done(((bf16[192,256]{1,0:T(8,128)(2,1)}), bf16[3072,256]{1,0:T(8,128)(2,1)}) %all-gather.13.cloned.1.call-update) | async-done | bytes 1572880 | tf_op jit(solution)/shard_map/all_gather | solution.py:154
  455.4 4.7 collective-permute-start.27
  467.0 15.4 %collective-permute-start.29 = (bf16[192,16]{1,0:T(8,128)(2,1)S(1)}, bf16[192,16]{1,0:T(8,128)(2,1)S(1)}, u32[]{:S(2)}, u32[]{:S(2)}) collective-permute-start(bf16[192,16]{1,0:T(8,128)(2,1)S(1)} %select_convert_fusion.4), channel_id=1, source_target_pairs={{0,1},{1,0},{2,3},{3,2},{4,5},{5,4},{6,7},{7,6},{8,9},{9,8},{10,11... | collective-permute-start | bytes 18440 | tf_op jit(solution)/shard_map/ppermute | solution.py:10
  491.5 4.7 collective-permute-start.32
  503.5 22.2 %scatter_fusion.4 = bf16[16,24,256]{2,1,0:T(8,128)(2,1)} fusion(bf16[16,24,256]{2,1,0:T(8,128)(2,1)} %broadcast.1392.clone.1, s32[192]{0:T(256)S(1)} %bitcast.316, bf16[192,256]{1,0:T(8,128)(2,1)S(1)} %maximum_select_fusion.4), kind=kCustom, calls=%fused_computation.14 | custom fusion | bytes 296448 | tf_op jit(solution)/shard_map/scatter | solution.py:48
  525.7 7.5 all-to-all-start.4
  538.0 4.9 collective-permute-start.34
  542.9 4.5 collective-permute-start.2
  548.1 22.1 %scatter_fusion.5 = bf16[16,24,256]{2,1,0:T(8,128)(2,1)} fusion(bf16[16,24,256]{2,1,0:T(8,128)(2,1)} %broadcast.1392.clone, s32[192]{0:T(256)S(1)} %bitcast.315, bf16[192,256]{1,0:T(8,128)(2,1)S(1)} %collective-permute-done.34), kind=kCustom, calls=%fused_computation.16 | custom fusion | bytes 296448 | tf_op jit(solution)/shard_map/scatter | solution.py:48
  570.2 11.7 all-to-all-start.5
  582.4 11.8 scatter_custom_fusion.12
  596.6 11.8 scatter_custom_fusion.17
  618.9 65.8 %all-gather.15.cloned.1.call-done = bf16[2048,256]{0,1:T(8,128)(2,1)} async-done(((bf16[128,256]{0,1:T(8,128)(2,1)}), bf16[2048,256]{0,1:T(8,128)(2,1)}) %all-gather.15.cloned.1.call-update) | async-done | bytes 1048592 | tf_op jit(solution)/shard_map/all_gather | solution.py:154
  687.7 137.6 %all-reduce.8.cloned.1.call-done = bf16[256,256]{0,1:T(8,128)(2,1)} async-done(((bf16[256,256]{0,1:T(8,128)(2,1)}), bf16[256,256]{0,1:T(8,128)(2,1)}) %all-reduce.8.cloned.1.call-update) | async-done | bytes 131088 | tf_op jit(solution)/shard_map/psum | solution.py:216
  828.4 24.2 %all_to_all.45 = bf16[16,24,256]{2,1,0:T(8,128)(2,1)S(1)} all-to-all(bf16[16,24,256]{2,1,0:T(8,128)(2,1)S(1)} %bitcast.322), channel_id=1, replica_groups=mesh['row'=16,'col'=32] {'row'}, dimensions={0} | all-to-all | bytes 393216 | tf_op jit(solution)/shard_map/all_to_all | solution.py:203
  855.9 121.3 %all-reduce.10.cloned.1.call-done = bf16[192,256]{1,0:T(8,128)(2,1)} async-done(((bf16[192,256]{1,0:T(8,128)(2,1)}), bf16[192,256]{1,0:T(8,128)(2,1)}) %all-reduce.10.cloned.1.call-update) | async-done | bytes 98320 | tf_op jit(solution)/shard_map/psum | solution.py:212
  983.7 4.6 collective-permute-start.36
  995.3 15.2 %collective-permute-start.38 = (bf16[192,16]{1,0:T(8,128)(2,1)S(1)}, bf16[192,16]{1,0:T(8,128)(2,1)S(1)}, u32[]{:S(2)}, u32[]{:S(2)}) collective-permute-start(bf16[192,16]{1,0:T(8,128)(2,1)S(1)} %select_convert_fusion), channel_id=1, source_target_pairs={{0,1},{1,0},{2,3},{3,2},{4,5},{5,4},{6,7},{7,6},{8,9},{9,8},{10,11... | collective-permute-start | bytes 18440 | tf_op jit(solution)/shard_map/ppermute | solution.py:10
  1019.7 4.6 collective-permute-start.41
  1032.2 18.2 %all_to_all.46 = bf16[16,16,256]{2,1,0:T(8,128)(2,1)S(1)} all-to-all(bf16[16,16,256]{2,1,0:T(8,128)(2,1)S(1)} %bitcast.327), channel_id=1, replica_groups=mesh['row'=16,'col'=32] {'row'}, dimensions={0} | all-to-all | bytes 262144 | tf_op jit(solution)/shard_map/all_to_all | solution.py:203
  1052.5 123.0 %all-reduce.12.cloned.1.call-done = bf16[256,256]{0,1:T(8,128)(2,1)} async-done(((bf16[256,256]{0,1:T(8,128)(2,1)}), bf16[256,256]{0,1:T(8,128)(2,1)}) %all-reduce.12.cloned.1.call-update) | async-done | bytes 131088 | tf_op jit(solution)/shard_map/psum | solution.py:212
  1176.6 4.6 collective-permute-start.43
  1187.3 13.9 %collective-permute-start.45 = (bf16[128,32]{0,1:T(8,128)(2,1)S(1)}, bf16[128,32]{0,1:T(8,128)(2,1)S(1)}, u32[]{:S(2)}, u32[]{:S(2)}) collective-permute-start(bf16[128,32]{0,1:T(8,128)(2,1)S(1)} %select_convert_fusion.16), channel_id=1, source_target_pairs={{0,1},{1,0},{2,3},{3,2},{4,5},{5,4},{6,7},{7,6},{8,9},{9,8},{10,11... | collective-permute-start | bytes 24584 | tf_op jit(solution)/shard_map/ppermute | solution.py:10
  1209.6 4.6 collective-permute-start.48
  1216.8 19.0 %all_to_all.47 = bf16[16,8,256]{2,1,0:T(8,128)(2,1)S(1)} all-to-all(bf16[16,8,256]{2,1,0:T(8,128)(2,1)S(1)} %bitcast.328), channel_id=1, replica_groups=mesh['row'=16,'col'=32] {'row'}, dimensions={0} | all-to-all | bytes 131072 | tf_op jit(solution)/shard_map/all_to_all | solution.py:203
  1237.6 120.9 %all-reduce.14.cloned.1.call-done = bf16[256,256]{0,1:T(8,128)(2,1)} async-done(((bf16[256,256]{0,1:T(8,128)(2,1)}), bf16[256,256]{0,1:T(8,128)(2,1)}) %all-reduce.14.cloned.1.call-update) | async-done | bytes 131088 | tf_op jit(solution)/shard_map/psum | solution.py:212
  1364.5 12.4 collective-permute-start.50
  (381 shorter events, 228.8 us)
Async XLA Ops:
  7.2 85.7 %all-gather.9.cloned.1.call-start = ((), (), s32[]{:S(2)}) async-start(), calls=%async_computation.13 | async-start | bytes 2228224 | tf_op jit(solution)/shard_map/all_gather | solution.py:154
  7.2 9.8 collective-permute-start.5
  24.1 118.5 %collective-permute-start.12 = (bf16[128,32]{0,1:T(8,128)(2,1)}, bf16[128,32]{0,1:T(8,128)(2,1)S(1)}, u32[]{:S(2)}, u32[]{:S(2)}) collective-permute-start(bf16[128,32]{0,1:T(8,128)(2,1)} %param.23), channel_id=1, source_target_pairs={{0,1},{1,0},{2,3},{3,2},{4,5},{5,4},{6,7},{7,6},{8,9},{9,8},{10,11... | collective-permute-start | bytes 24584 | tf_op jit(solution)/shard_map/ppermute | solution.py:10
  101.1 18.1 %collective-permute-start.8 = (bf16[64,64]{1,0:T(8,128)(2,1)S(1)}, bf16[64,64]{1,0:T(8,128)(2,1)S(1)}, u32[]{:S(2)}, u32[]{:S(2)}) collective-permute-start(bf16[64,64]{1,0:T(8,128)(2,1)S(1)} %select_convert_fusion.14), channel_id=1, source_target_pairs={{0,1},{1,0},{2,3},{3,2},{4,5},{5,4},{6,7},{7,6},{8,9},{9,8},{10,11... | collective-permute-start | bytes 24584 | tf_op jit(solution)/shard_map/ppermute | solution.py:10
  135.3 27.6 %all-to-all-start = ((bf16[16,8,256]{2,1,0:T(8,128)(2,1)}), bf16[16,8,256]{2,1,0:T(8,128)(2,1)S(1)}, u32[]{:S(2)}, u32[]{:S(2)}) async-start(bf16[16,8,256]{2,1,0:T(8,128)(2,1)} %scatter_fusion), calls=%async_computation | async-start | bytes 131072 | tf_op jit(solution)/shard_map/all_to_all | solution.py:170
  142.5 32.0 %collective-permute-start.13 = (bf16[128,64]{0,1:T(8,128)(2,1)S(1)}, bf16[128,64]{0,1:T(8,128)(2,1)S(1)}, u32[]{:S(2)}, u32[]{:S(2)}) collective-permute-start(bf16[128,64]{0,1:T(8,128)(2,1)S(1)} %maximum_select_fusion.28), channel_id=1, source_target_pairs={{0,2},{1,3},{2,0},{3,1},{4,6},{5,7},{6,4},{7,5},{8,10},{9,11},{10,... | collective-permute-start | bytes 49160 | tf_op jit(solution)/shard_map/ppermute | solution.py:10
  145.7 8.9 collective-permute-start.11
  162.8 23.2 %all-to-all-start.1 = ((bf16[16,8,256]{2,1,0:T(8,128)(2,1)}), bf16[16,8,256]{2,1,0:T(8,128)(2,1)S(1)}, u32[]{:S(2)}, u32[]{:S(2)}) async-start(bf16[16,8,256]{2,1,0:T(8,128)(2,1)} %scatter_fusion.1), calls=%async_computation.1 | async-start | bytes 131072 | tf_op jit(solution)/shard_map/all_to_all | solution.py:177
  174.5 78.6 %all-gather.11.cloned.1.call-start = ((), (), s32[]{:S(2)}) async-start(), calls=%async_computation.14 | async-start | bytes 2228224 | tf_op jit(solution)/shard_map/all_gather | solution.py:154
  174.5 13.2 collective-permute-start.14
  188.6 146.1 %collective-permute-start.22 = (bf16[192,16]{0,1:T(8,128)(2,1)S(1)}, bf16[192,16]{0,1:T(8,128)(2,1)S(1)}, u32[]{:S(2)}, u32[]{:S(2)}) collective-permute-start(bf16[192,16]{0,1:T(8,128)(2,1)S(1)} %copy-done.11), channel_id=1, source_target_pairs={{0,1},{1,0},{2,3},{3,2},{4,5},{5,4},{6,7},{7,6},{8,9},{9,8},{10,11... | collective-permute-start | bytes 18440 | tf_op jit(solution)/shard_map/ppermute | solution.py:10
  194.5 338.8 %collective-permute-start = (bf16[256,8]{0,1:T(8,128)(2,1)S(1)}, bf16[256,8]{0,1:T(8,128)(2,1)S(1)}, u32[]{:S(2)}, u32[]{:S(2)}) collective-permute-start(bf16[256,8]{0,1:T(8,128)(2,1)S(1)} %copy-done.12), channel_id=1, source_target_pairs={{0,1},{1,0},{2,3},{3,2},{4,5},{5,4},{6,7},{7,6},{8,9},{9,8},{10,11... | collective-permute-start | bytes 12296 | tf_op jit(solution)/shard_map/ppermute | solution.py:10
  256.7 6.2 collective-permute-start.15
  267.4 15.6 %collective-permute-start.17 = (bf16[128,32]{0,1:T(8,128)(2,1)S(1)}, bf16[128,32]{0,1:T(8,128)(2,1)S(1)}, u32[]{:S(2)}, u32[]{:S(2)}) collective-permute-start(bf16[128,32]{0,1:T(8,128)(2,1)S(1)} %select_convert_fusion.17), channel_id=1, source_target_pairs={{0,1},{1,0},{2,3},{3,2},{4,5},{5,4},{6,7},{7,6},{8,9},{9,8},{10,11... | collective-permute-start | bytes 24584 | tf_op jit(solution)/shard_map/ppermute | solution.py:10
  290.6 12.9 collective-permute-start.20
  319.3 37.0 %all-to-all-start.2 = ((bf16[16,16,256]{2,1,0:T(8,128)(2,1)}), bf16[16,16,256]{2,1,0:T(8,128)(2,1)S(1)}, u32[]{:S(2)}, u32[]{:S(2)}) async-start(bf16[16,16,256]{2,1,0:T(8,128)(2,1)} %scatter_fusion.2), calls=%async_computation.2 | async-start | bytes 262144 | tf_op jit(solution)/shard_map/all_to_all | solution.py:170
  335.0 5.5 collective-permute-start.21
  338.2 29.6 %collective-permute-start.23 = (bf16[192,32]{1,0:T(8,128)(2,1)S(1)}, bf16[192,32]{1,0:T(8,128)(2,1)S(1)}, u32[]{:S(2)}, u32[]{:S(2)}) collective-permute-start(bf16[192,32]{1,0:T(8,128)(2,1)S(1)} %broadcast_select_fusion.1), channel_id=1, source_target_pairs={{0,2},{1,3},{2,0},{3,1},{4,6},{5,7},{6,4},{7,5},{8,10},{9,11},{10,... | collective-permute-start | bytes 36872 | tf_op jit(solution)/shard_map/ppermute | solution.py:10
  356.2 23.5 %all-to-all-start.3 = ((bf16[16,16,256]{2,1,0:T(8,128)(2,1)}), bf16[16,16,256]{2,1,0:T(8,128)(2,1)S(1)}, u32[]{:S(2)}, u32[]{:S(2)}) async-start(bf16[16,16,256]{2,1,0:T(8,128)(2,1)} %scatter_fusion.3), calls=%async_computation.3 | async-start | bytes 262144 | tf_op jit(solution)/shard_map/all_to_all | solution.py:177
  367.8 80.5 %all-gather.13.cloned.1.call-start = ((), (), s32[]{:S(2)}) async-start(), calls=%async_computation.15 | async-start | bytes 1671168 | tf_op jit(solution)/shard_map/all_gather | solution.py:154
  368.0 6.3 collective-permute-start.24
  374.4 7.5 collective-permute-start.25
  450.1 5.2 collective-permute-start.26
  455.4 6.3 collective-permute-start.27
  467.0 16.3 %collective-permute-start.29 = (bf16[192,16]{1,0:T(8,128)(2,1)S(1)}, bf16[192,16]{1,0:T(8,128)(2,1)S(1)}, u32[]{:S(2)}, u32[]{:S(2)}) collective-permute-start(bf16[192,16]{1,0:T(8,128)(2,1)S(1)} %select_convert_fusion.4), channel_id=1, source_target_pairs={{0,1},{1,0},{2,3},{3,2},{4,5},{5,4},{6,7},{7,6},{8,9},{9,8},{10,11... | collective-permute-start | bytes 18440 | tf_op jit(solution)/shard_map/ppermute | solution.py:10
  491.5 6.3 collective-permute-start.32
  498.0 4.8 collective-permute-start.33
  525.7 44.5 %all-to-all-start.4 = ((bf16[16,24,256]{2,1,0:T(8,128)(2,1)}), bf16[16,24,256]{2,1,0:T(8,128)(2,1)S(1)}, u32[]{:S(2)}, u32[]{:S(2)}) async-start(bf16[16,24,256]{2,1,0:T(8,128)(2,1)} %scatter_fusion.4), calls=%async_computation.4 | async-start | bytes 393216 | tf_op jit(solution)/shard_map/all_to_all | solution.py:170
  538.0 9.4 collective-permute-start.34
  542.9 51.4 %collective-permute-start.2 = (bf16[256,32]{1,0:T(8,128)(2,1)S(1)}, bf16[256,32]{1,0:T(8,128)(2,1)S(1)}, u32[]{:S(2)}, u32[]{:S(2)}) collective-permute-start(bf16[256,32]{1,0:T(8,128)(2,1)S(1)} %broadcast_select_fusion), channel_id=1, source_target_pairs={{0,4},{1,5},{2,6},{3,7},{4,0},{5,1},{6,2},{7,3},{8,12},{9,13},{10,... | collective-permute-start | bytes 49160 | tf_op jit(solution)/shard_map/ppermute | solution.py:10
  570.2 44.9 %all-to-all-start.5 = ((bf16[16,24,256]{2,1,0:T(8,128)(2,1)}), bf16[16,24,256]{2,1,0:T(8,128)(2,1)S(1)}, u32[]{:S(2)}, u32[]{:S(2)}) async-start(bf16[16,24,256]{2,1,0:T(8,128)(2,1)} %scatter_fusion.5), calls=%async_computation.5 | async-start | bytes 393216 | tf_op jit(solution)/shard_map/all_to_all | solution.py:177
  581.9 102.8 %all-gather.15.cloned.1.call-start = ((), (), s32[]{:S(2)}) async-start(), calls=%async_computation.16 | async-start | bytes 1114112 | tf_op jit(solution)/shard_map/all_gather | solution.py:154
  594.4 14.1 %collective-permute-start.3 = (bf16[256,64]{1,0:T(8,128)(2,1)S(1)}, bf16[256,64]{1,0:T(8,128)(2,1)S(1)}, u32[]{:S(2)}, u32[]{:S(2)}) collective-permute-start(bf16[256,64]{1,0:T(8,128)(2,1)S(1)} %maximum_select_fusion.6), channel_id=1, source_target_pairs={{0,8},{1,9},{2,10},{3,11},{4,12},{5,13},{6,14},{7,15},{8,0},{9,1},... | collective-permute-start | bytes 98312 | tf_op jit(solution)/shard_map/ppermute | solution.py:10
  608.6 9.3 collective-permute-start.4
  618.9 206.5 %all-reduce.8.cloned.1.call-start = ((), (), s32[]{:S(2)}) async-start(), calls=%async_computation.9 | async-start | bytes 262144 | tf_op jit(solution)/shard_map/psum | solution.py:216
  687.6 289.6 %all-reduce.10.cloned.1.call-start = ((), (), s32[]{:S(2)}) async-start(), calls=%async_computation.10 | async-start | bytes 196608 | tf_op jit(solution)/shard_map/psum | solution.py:212
  855.9 319.6 %all-reduce.12.cloned.1.call-start = ((), (), s32[]{:S(2)}) async-start(), calls=%async_computation.11 | async-start | bytes 262144 | tf_op jit(solution)/shard_map/psum | solution.py:212
  978.4 5.2 collective-permute-start.35
  983.7 6.3 collective-permute-start.36
  995.3 16.1 %collective-permute-start.38 = (bf16[192,16]{1,0:T(8,128)(2,1)S(1)}, bf16[192,16]{1,0:T(8,128)(2,1)S(1)}, u32[]{:S(2)}, u32[]{:S(2)}) collective-permute-start(bf16[192,16]{1,0:T(8,128)(2,1)S(1)} %select_convert_fusion), channel_id=1, source_target_pairs={{0,1},{1,0},{2,3},{3,2},{4,5},{5,4},{6,7},{7,6},{8,9},{9,8},{10,11... | collective-permute-start | bytes 18440 | tf_op jit(solution)/shard_map/ppermute | solution.py:10
  1019.7 6.3 collective-permute-start.41
  1026.1 4.8 collective-permute-start.42
  1052.5 305.9 %all-reduce.14.cloned.1.call-start = ((), (), s32[]{:S(2)}) async-start(), calls=%async_computation.12 | async-start | bytes 262144 | tf_op jit(solution)/shard_map/psum | solution.py:212
  1176.6 6.2 collective-permute-start.43
  1187.3 14.7 %collective-permute-start.45 = (bf16[128,32]{0,1:T(8,128)(2,1)S(1)}, bf16[128,32]{0,1:T(8,128)(2,1)S(1)}, u32[]{:S(2)}, u32[]{:S(2)}) collective-permute-start(bf16[128,32]{0,1:T(8,128)(2,1)S(1)} %select_convert_fusion.16), channel_id=1, source_target_pairs={{0,1},{1,0},{2,3},{3,2},{4,5},{5,4},{6,7},{7,6},{8,9},{9,8},{10,11... | collective-permute-start | bytes 24584 | tf_op jit(solution)/shard_map/ppermute | solution.py:10
  1209.6 6.2 collective-permute-start.48
  1359.5 4.9 collective-permute-start.49
  1364.5 14.3 %collective-permute-start.50 = (bf16[64,64]{1,0:T(8,128)(2,1)S(1)}, bf16[64,64]{1,0:T(8,128)(2,1)S(1)}, u32[]{:S(2)}, u32[]{:S(2)}) collective-permute-start(bf16[64,64]{1,0:T(8,128)(2,1)S(1)} %select_convert_fusion.10), channel_id=1, source_target_pairs={{0,1},{1,0},{2,3},{3,2},{4,5},{5,4},{6,7},{7,6},{8,9},{9,8},{10,11... | collective-permute-start | bytes 24584 | tf_op jit(solution)/shard_map/ppermute | solution.py:10
  (35 other events, 1519.3 us)
Sparse Core Ops, SparseCore 0:
  24.2 68.6 all-gather.8
  188.7 64.2 all-gather.10
  382.8 65.3 all-gather.12
  619.0 65.7 all-gather.14
  687.8 137.4 all-reduce.7
  856.0 121.2 all-reduce.9
  1052.6 122.8 all-reduce.11
  1237.7 120.6 all-reduce.13
